TPU v7x, 32 devices: a whole 2x2x4 slice. The times are simulated.
32 devices in a mesh: groups: 2 (over y), span: 2 (over x), tok: 4 (over z), head: 2 (over core).
Axes of the slice: x: 2, y: 2, z: 4, core: 2. Of those that a mesh axis runs over, the one named last changes fastest.
Arguments:
- queries: bfloat16 [16384, 2, 256], P(('groups', 'span', 'tok'), 'head'), parts along dimension 0, may hold values from -6 to 6
- keys: bfloat16 [16384, 2, 256], P(('groups', 'span', 'tok'), 'head'), parts along dimension 0, may hold values from -6 to 6
- values: bfloat16 [16384, 2, 256], P(('groups', 'span', 'tok'), 'head'), parts along dimension 0, may hold values from -6 to 6
- rates: float32 [16384, 2], P(('groups', 'span', 'tok'), 'head'), parts along dimension 0, may hold values from 0.0001 to 0.001
- w_in: bfloat16 [2, 2, 256, 256], P('head'), may hold values from -0.375 to 0.375
- w_out: bfloat16 [2, 256, 256], P('head'), may hold values from -0.375 to 0.375
- gain: float32 [2, 256], P('head'), may hold values from 0.1 to 1.9
- block_doc: int32 [128], P('groups'), parts along dimension 0, may hold values from 0 to 15, never falling along the last dimension, each value on 1 to 8 neighbouring positions
Outputs:
- mixed: bfloat16 [16384, 2, 256], P(('groups', 'span', 'tok'), 'head'), parts along dimension 0
There are 2 independent parts, one for each index of `groups`. A program takes and returns all parts, laid end to end along the dimension named above; an argument that names none is the same for every part. Nothing has to cross between parts.
Inputs may be any that keep to these rules, and one draw needn't show every extreme that they name: block_doc never falls from one block to the next; each document covers 1 to 8 consecutive blocks, one exactly 8.
All inputs are finite; a program needn't handle non-finite values.
Results may differ from a plain program's by a relative error of at most 0.01.
Values may be sent and summed in bfloat16 or wider, within the bound.
A program may use at most 64 MiB of HBM per device.

v0:
```python
import math
import jax
import jax.numpy as jnp
from jax import lax
from jax.sharding import PartitionSpec as P

BLOCK = 128
EPSILON = 1e-06


def from_behind(block, axis, distance):
    devices = range(lax.axis_size(axis))
    route = [(i - distance, i) for i in devices if i - distance in devices]
    return lax.ppermute(block, axis, route)


def rms_scale(inputs):
    return inputs * lax.rsqrt(jnp.mean(inputs * inputs, axis=-1, keepdims=True) + EPSILON)


def silu_slope(pre):
    sigmoid_val = jax.nn.sigmoid(pre)
    return sigmoid_val * (1.0 + pre * (1.0 - sigmoid_val))


def renormalize(updated, row_norm):
    scale = row_norm * lax.rsqrt(jnp.sum(updated * updated, axis=-1, keepdims=True) + EPSILON)
    return (updated * scale).astype(jnp.bfloat16)


def local_gradient(keys_norm, values, rates, w_in, w_out):
    gate_pre = jnp.einsum("thd,hfd->thf", keys_norm, w_in[:, 0], preferred_element_type=jnp.float32)
    up_pre = jnp.einsum("thd,hfd->thf", keys_norm, w_in[:, 1], preferred_element_type=jnp.float32)
    activation = (jax.nn.silu(gate_pre) * up_pre).astype(jnp.bfloat16)
    target = (-(rates[:, :, None] * values.astype(jnp.float32))).astype(jnp.bfloat16)
    act_grad = jnp.einsum("thd,hdf->thf", target, w_out, preferred_element_type=jnp.float32)
    gate_grad = (act_grad * up_pre * silu_slope(gate_pre)).astype(jnp.bfloat16)
    up_grad = (act_grad * jax.nn.silu(gate_pre)).astype(jnp.bfloat16)
    stacked = jnp.stack([gate_grad, up_grad], axis=1)
    grad_in = jnp.einsum("tchf,thd->hcfd", stacked, keys_norm, preferred_element_type=jnp.float32)
    grad_out = jnp.einsum("thd,thf->hdf", target, activation, preferred_element_type=jnp.float32)
    return (grad_in, grad_out)


def attend_blocks(query_norm, keys_norm, values, prior_keys, prior_values, prior_open):
    tokens, heads, width = query_norm.shape
    block_count = tokens // BLOCK
    shape = (block_count, BLOCK, heads, width)
    window_keys = jnp.concatenate([prior_keys.reshape(shape), keys_norm.reshape(shape)], axis=1)
    window_values = jnp.concatenate([prior_values.reshape(shape), values.reshape(shape)], axis=1)
    scores = jnp.einsum(
        "nqhd,nkhd->nhqk",
        query_norm.reshape(shape),
        window_keys,
        preferred_element_type=jnp.float32,
    ) / math.sqrt(width)
    row_pos = lax.broadcasted_iota(jnp.int32, (BLOCK, 2 * BLOCK), 0)
    col_pos = lax.broadcasted_iota(jnp.int32, (BLOCK, 2 * BLOCK), 1)
    inside = col_pos - BLOCK <= row_pos
    visible = jnp.where(col_pos[None] < BLOCK, prior_open[:, None, None], inside[None])
    weights = jnp.where(visible[:, None], jnp.exp(scores), 0.0)
    probabilities = (weights / jnp.sum(weights, axis=-1, keepdims=True)).astype(jnp.bfloat16)
    attended = jnp.einsum(
        "nhqk,nkhd->nqhd", probabilities, window_values, preferred_element_type=jnp.float32
    )
    return attended.reshape(tokens, heads, width)


def body(queries, keys, values, rates, w_in, w_out, gain, block_doc):
    query_norm = rms_scale(queries.astype(jnp.float32)).astype(jnp.bfloat16)
    keys_norm = rms_scale(keys.astype(jnp.float32)).astype(jnp.bfloat16)
    span_pos = lax.axis_index("span")
    span_count = lax.axis_size("span")
    tok_pos = lax.axis_index("tok")
    tok_count = lax.axis_size("tok")
    norm_in = jnp.sqrt(jnp.sum(jnp.square(w_in.astype(jnp.float32)), axis=-1, keepdims=True))
    norm_out = jnp.sqrt(jnp.sum(jnp.square(w_out.astype(jnp.float32)), axis=-1, keepdims=True))
    zeros_in = jnp.zeros(w_in.shape, jnp.float32)
    zeros_out = jnp.zeros(w_out.shape, jnp.float32)
    hidden_rows = w_in.shape[2] // tok_count
    feature_rows = w_out.shape[1] // tok_count

    def shard_of(full_in, full_out):
        return (
            lax.dynamic_slice_in_dim(full_in, tok_pos * hidden_rows, hidden_rows, 2),
            lax.dynamic_slice_in_dim(full_out, tok_pos * feature_rows, feature_rows, 1),
        )

    part_norm_in, part_norm_out = shard_of(norm_in, norm_out)

    def gradient_at(link_step, full_in, full_out):
        return lax.cond(
            span_pos == link_step,
            lambda: local_gradient(keys_norm, values, rates, full_in, full_out),
            lambda: (zeros_in, zeros_out),
        )

    def advance(link_step, state_carry):
        full_in, full_out, own_in, own_out = state_carry
        grad_in, grad_out = gradient_at(link_step, full_in, full_out)
        sum_in, sum_out = (
            lax.psum_scatter(
                grad_in.astype(jnp.bfloat16), "tok", scatter_dimension=2, tiled=True
            ).astype(jnp.float32),
            lax.psum_scatter(
                grad_out.astype(jnp.bfloat16), "tok", scatter_dimension=1, tiled=True
            ).astype(jnp.float32),
        )
        new_in = renormalize(own_in.astype(jnp.float32) - sum_in, part_norm_in)
        new_out = renormalize(own_out.astype(jnp.float32) - sum_out, part_norm_out)
        got_in, got_out = from_behind((new_in, new_out), "span", 1)
        receiver = span_pos == link_step + 1
        own_in = jnp.where(receiver, got_in, own_in)
        own_out = jnp.where(receiver, got_out, own_out)
        full_in, full_out = (
            lax.all_gather(own_in, "tok", axis=2, tiled=True),
            lax.all_gather(own_out, "tok", axis=1, tiled=True),
        )
        return (full_in, full_out, own_in, own_out)

    start_in, start_out = shard_of(w_in, w_out)
    fast_in, fast_out_w, last_in, last_out = lax.fori_loop(
        0, span_count - 1, advance, (w_in, w_out, start_in, start_out)
    )
    gate_pre = jnp.einsum(
        "thd,hfd->thf", query_norm, fast_in[:, 0], preferred_element_type=jnp.float32
    )
    up_pre = jnp.einsum(
        "thd,hfd->thf", query_norm, fast_in[:, 1], preferred_element_type=jnp.float32
    )
    activation = (jax.nn.silu(gate_pre) * up_pre).astype(jnp.bfloat16)
    fast_output = jnp.einsum(
        "thf,hdf->thd", activation, fast_out_w, preferred_element_type=jnp.float32
    )
    ttt = rms_scale(fast_output) * gain[None]
    before_keys, before_values = from_behind(
        (keys_norm[-BLOCK:], values[-BLOCK:]), ("span", "tok"), 1
    )
    prior_keys = jnp.concatenate([before_keys, keys_norm[:-BLOCK]], axis=0)
    prior_values = jnp.concatenate([before_values, values[:-BLOCK]], axis=0)
    block_count = queries.shape[0] // BLOCK
    device_index = span_pos * tok_count + tok_pos
    padded_docs = jnp.concatenate([jnp.full((1,), -1, jnp.int32), block_doc])
    block_start = device_index * block_count
    prior_docs = lax.dynamic_slice_in_dim(padded_docs, block_start, block_count)
    own_docs = lax.dynamic_slice_in_dim(padded_docs, block_start + 1, block_count)
    prior_open = prior_docs == own_docs
    attended = attend_blocks(query_norm, keys_norm, values, prior_keys, prior_values, prior_open)
    return (attended + ttt).astype(jnp.bfloat16)


def solution(mesh):
    placed = (
        P(("groups", "span", "tok"), "head", None),
        P(("groups", "span", "tok"), "head", None),
        P(("groups", "span", "tok"), "head", None),
        P(("groups", "span", "tok"), "head"),
        P("head", None, None, None),
        P("head", None, None),
        P("head", None),
        P("groups"),
    )
    return jax.shard_map(
        body,
        mesh=mesh,
        in_specs=placed,
        out_specs=P(("groups", "span", "tok"), "head", None),
        check_vma=False,
    )
```

profile of v0, /device:TPU:0, one launch (start us, length us, event | category | flops | bytes accessed | tf_op | source)
XLA Modules:
  0.0 98.3 jit_solution(1689548513804843051)
XLA Ops:
  6.6 1.3 %fusion.28 = f32[1024]{0:T(1024)S(1)} fusion(bf16[1024,1,256]{2,0,1:T(8,128)(2,1)} %param.11), kind=kLoop, calls=%fused_computation.43 | loop fusion | flops 785408 | bytes 528384 | tf_op jit(solution)/shard_map/reduce_sum | solution.py:18
  7.9 1.2 %fusion.29 = bf16[1024,1,256]{2,0,1:T(8,128)(2,1)S(1)} fusion(bf16[1024,1,256]{2,0,1:T(8,128)(2,1)} %param.11, f32[1024]{0:T(1024)S(1)} %add_rsqrt_fusion.1), kind=kLoop, calls=%fused_computation.44 | loop fusion | flops 786432 | bytes 1052672 | tf_op jit(solution)/shard_map/convert_element_type | solution.py:71
  9.2 2.6 %conditional.1 = (bf16[1,2,256,256]{3,2,1,0:T(8,128)(2,1)S(1)}, bf16[1,256,256]{2,1,0:T(8,128)(2,1)S(1)}) conditional(s32[]{:T(128)} %convert_element_type.85, () %tuple.15, (f32[1024,1]{0,1:T(1,128)S(1)}, bf16[1024,1,256]{2,0,1:T(8,128)(2,1)S(1)}, bf16[1,256,256]{2,1,0:T(8,128)(2,1)S(1)}, bf16[1,2,256,256]{3,2,1,0:T(8,128)(2,1)S(1)}, ...), branch_computations={%region_3.0_spmd, %region_4.5_spmd} | conditional | flops 812908544 | bytes 11804688 | solution.py:92
  9.2 0.3 convolution_bitcast_fusion
  9.6 0.3 convolution_bitcast_fusion.1
  9.9 0.7 fusion.10
  10.6 0.5 convolution_bitcast_fusion.3
  11.1 0.6 convolution_bitcast_fusion.4
  11.8 0.6 copy-done.5
  12.5 4.9 %collective-permute-start.1 = (bf16[128,1,256]{2,0,1:T(8,128)(2,1)S(1)}, bf16[128,1,256]{2,0,1:T(8,128)(2,1)S(1)}, u32[]{:S(2)}, u32[]{:S(2)}) collective-permute-start(bf16[128,1,256]{2,0,1:T(8,128)(2,1)S(1)} %slice.30), channel_id=1, source_target_pairs={{0,2},{2,4},{4,6},{6,8},{8,10},{10,12},{12,14},{1,3},{3,5},{5,7},{... | collective-permute-start | bytes 196616 | tf_op jit(solution)/shard_map/ppermute | solution.py:14
  17.5 3.5 %collective-permute-start = (bf16[128,1,256]{2,0,1:T(8,128)(2,1)S(1)}, bf16[128,1,256]{2,0,1:T(8,128)(2,1)S(1)}, u32[]{:S(2)}, u32[]{:S(2)}) collective-permute-start(bf16[128,1,256]{2,0,1:T(8,128)(2,1)S(1)} %slice.24), channel_id=1, source_target_pairs={{0,2},{2,4},{4,6},{6,8},{8,10},{10,12},{12,14},{1,3},{3,5},{5,7},{... | collective-permute-start | bytes 196616 | tf_op jit(solution)/shard_map/ppermute | solution.py:14
  21.4 0.8 copy-done
  22.2 0.2 fusion.26
  22.4 0.2 fusion.27
  22.9 1.5 %fusion.23 = f32[8,128,256]{2,1,0:T(8,128)} fusion(bf16[8,128,256]{2,1,0:T(8,128)(2,1)S(1)} %bitcast.130, bf16[8,128,1,256]{3,1,0,2:T(8,128)(2,1)S(1)} %bitcast.129, bf16[8,128,1,256]{3,1,0,2:T(8,128)(2,1)S(1)} %bitcast.133, pred[128,256]{1,0:T(8,128)(4,1)S(1)} %get-tuple-element.71, pred[128,256]{1,0:T(8,128)(4,1)S(1)} %get-tuple-element.72, ...), kind=kOutput, calls=%fused_computation.34 | convolution fusion | flops 137101312 | bytes 2686984 | tf_op jit(solution)/shard_map/nqhd,nkhd->nhqk/dot_general | solution.py:51
  24.5 1.0 %copy-done.4 = bf16[1024,1,256]{2,0,1:T(8,128)(2,1)S(1)} copy-done((bf16[1024,1,256]{2,0,1:T(8,128)(2,1)S(1)}, bf16[1024,1,256]{2,0,1:T(8,128)(2,1)}, u32[]{:S(2)}) %copy-start.4) | copy-done | bytes 524312
  25.5 1.9 %fusion.32 = f32[8,256,128]{1,2,0:T(8,128)S(1)} fusion(bf16[8,128,1,256]{3,1,0,2:T(8,128)(2,1)S(1)} %bitcast.132, bf16[8,128,1,256]{3,1,0,2:T(8,128)(2,1)S(1)} %bitcast.134, f32[8,128,256]{2,1,0:T(8,128)} %fusion.23), kind=kOutput, calls=%fused_computation.49 | convolution fusion | flops 136840448 | bytes 3145728 | tf_op jit(solution)/shard_map/nhqk,nkhd->nqhd/dot_general | solution.py:63
  27.4 0.3 copy.19
  27.7 5.8 %reduce-scatter.3.cloned.1.call-done = bf16[1,64,256]{2,1,0:T(8,128)(2,1)} async-done(((bf16[1,256,256]{2,1,0:T(8,128)(2,1)}), bf16[1,64,256]{2,1,0:T(8,128)(2,1)}) %reduce-scatter.3.cloned.1.call-update) | async-done | bytes 32784 | tf_op jit(solution)/shard_map/while/body/eval_jaxpr/reduce_scatter | solution.py:105
  33.6 0.9 multiply_reduce_fusion.4
  34.5 0.8 multiply_convert_fusion.4
  35.4 3.3 %collective-permute-start.2 = (bf16[1,64,256]{2,1,0:T(8,128)(2,1)S(1)}, bf16[1,64,256]{2,1,0:T(8,128)(2,1)S(1)}, u32[]{:S(2)}, u32[]{:S(2)}) collective-permute-start(bf16[1,64,256]{2,1,0:T(8,128)(2,1)S(1)} %multiply_convert_fusion.4), channel_id=1, source_target_pairs={{0,8},{1,9},{2,10},{3,11},{4,12},{5,13},{6,14},{7,15},{16,24},{17,... | collective-permute-start | bytes 98312 | tf_op jit(solution)/shard_map/while/body/eval_jaxpr/ppermute | solution.py:14
  38.7 14.9 %reduce-scatter.5.cloned.1.call-done = bf16[1,2,64,256]{3,2,1,0:T(8,128)(2,1)} async-done(((bf16[1,2,256,256]{3,2,1,0:T(8,128)(2,1)}), bf16[1,2,64,256]{3,2,1,0:T(8,128)(2,1)}) %reduce-scatter.5.cloned.1.call-update) | async-done | bytes 65552 | tf_op jit(solution)/shard_map/while/body/eval_jaxpr/reduce_scatter | solution.py:102
  53.6 0.9 multiply_reduce_fusion.3
  54.6 0.9 multiply_convert_fusion.3
  55.6 3.5 %collective-permute-start.3 = (bf16[1,2,64,256]{3,2,1,0:T(8,128)(2,1)S(1)}, bf16[1,2,64,256]{3,2,1,0:T(8,128)(2,1)S(1)}, u32[]{:S(2)}, u32[]{:S(2)}) collective-permute-start(bf16[1,2,64,256]{3,2,1,0:T(8,128)(2,1)S(1)} %multiply_convert_fusion.3), channel_id=1, source_target_pairs={{0,8},{1,9},{2,10},{3,11},{4,12},{5,13},{6,14},{7,15},{16,24},{17,... | collective-permute-start | bytes 196616 | tf_op jit(solution)/shard_map/while/body/eval_jaxpr/ppermute | solution.py:14
  59.1 13.5 %all_gather.8 = bf16[1,256,256]{2,1,0:T(8,128)(2,1)S(1)} all-gather(bf16[1,64,256]{2,1,0:T(8,128)(2,1)S(1)} %broadcast_select_fusion.1), channel_id=1, replica_groups=mesh['groups'=2,'span'=2,'tok'=4,'head'=2] {'tok'}, dimensions={1}, use_global_device_ids=true | all-gather | bytes 163840 | tf_op jit(solution)/shard_map/while/body/eval_jaxpr/all_gather | solution.py:117
  72.6 14.4 %all_gather.9 = bf16[1,2,256,256]{3,2,1,0:T(8,128)(2,1)S(1)} all-gather(bf16[1,2,64,256]{3,2,1,0:T(8,128)(2,1)S(1)} %broadcast_select_fusion), channel_id=1, replica_groups=mesh['groups'=2,'span'=2,'tok'=4,'head'=2] {'tok'}, dimensions={2}, use_global_device_ids=true | all-gather | bytes 327680 | tf_op jit(solution)/shard_map/while/body/eval_jaxpr/all_gather | solution.py:116
  87.0 1.3 %convolution_bitcast_fusion.7 = f32[1024,1,256]{0,2,1:T(8,128)} fusion(bf16[1024,1,256]{2,0,1:T(8,128)(2,1)S(1)} %fusion.27, bf16[1,2,256,256]{3,2,1,0:T(8,128)(2,1)S(1)} %all_gather.9), kind=kOutput, calls=%fused_computation.31 | convolution fusion | flops 134217728 | bytes 1703936 | tf_op jit(solution)/shard_map/thd,hfd->thf/dot_general | solution.py:125
  88.4 1.9 %multiply_reduce_fusion = (f32[1024]{0:T(1024)S(1)}, f32[1,256,1024]{2,1,0:T(8,128)S(1)}) fusion(f32[1024,1,256]{0,2,1:T(8,128)} %convolution_bitcast_fusion.7, bf16[1024,1,256]{2,0,1:T(8,128)(2,1)S(1)} %fusion.27, bf16[1,2,256,256]{3,2,1,0:T(8,128)(2,1)S(1)} %all_gather.9, bf16[1,256,256]{2,1,0:T(8,128)(2,1)S(1)} %all_gather.8), kind=kOutput, calls=%fused_computation.54 | convolution fusion | flops 270531584 | bytes 2887680 | tf_op jit(solution)/shard_map/thf,hdf->thd/dot_general | solution.py:132
  90.3 0.2 fusion.35
  90.5 1.0 %copy.20 = bf16[1024,1,256]{2,0,1:T(8,128)(2,1)} copy(bf16[1024,1,256]{0,2,1:T(8,128)(2,1)S(1)} %fusion.35) | data formatting | bytes 1048576 | tf_op jit(solution)/shard_map/convert_element_type | solution.py:149
  (47 shorter events, 1.0 us)
Async XLA Ops:
  6.5 2.7 %copy-start.3 = (bf16[1024,1,256]{2,0,1:T(8,128)(2,1)S(1)}, bf16[1024,1,256]{2,0,1:T(8,128)(2,1)}, u32[]{:S(2)}) copy-start(bf16[1024,1,256]{2,0,1:T(8,128)(2,1)} %param.12) | copy-start | bytes 1572868
  6.5 2.7 %copy-start.9 = (f32[1024,1]{0,1:T(1,128)S(1)}, f32[1024,1]{0,1:T(1,128)}, u32[]{:S(2)}) copy-start(f32[1024,1]{0,1:T(1,128)} %param.13) | copy-start | bytes 12292
  6.5 2.7 %copy-start.1 = (bf16[1,2,256,256]{3,2,1,0:T(8,128)(2,1)S(1)}, bf16[1,2,256,256]{3,2,1,0:T(8,128)(2,1)}, u32[]{:S(2)}) copy-start(bf16[1,2,256,256]{3,2,1,0:T(8,128)(2,1)} %param.14) | copy-start | bytes 786436
  6.5 2.7 %copy-start.6 = (bf16[1,256,256]{2,1,0:T(8,128)(2,1)S(1)}, bf16[1,256,256]{2,1,0:T(8,128)(2,1)}, u32[]{:S(2)}) copy-start(bf16[1,256,256]{2,1,0:T(8,128)(2,1)} %param.15) | copy-start | bytes 393220
  6.5 27.0 %reduce-scatter.3.cloned.1.call-start = ((), (), s32[]{:S(2)}) async-start(), calls=%async_computation.2 | async-start | bytes 163840 | tf_op jit(solution)/shard_map/while/body/eval_jaxpr/reduce_scatter | solution.py:105
  11.8 0.6 copy-start.5
  11.8 9.2 %copy-start.2 = (bf16[1,2,256,256]{3,2,1,0:T(8,128)(2,1)}, bf16[1,2,256,256]{3,2,1,0:T(8,128)(2,1)S(1)}, u32[]{:S(2)}) copy-start(bf16[1,2,256,256]{3,2,1,0:T(8,128)(2,1)S(1)} %get-tuple-element.45) | copy-start | bytes 786436
  12.5 41.1 %reduce-scatter.5.cloned.1.call-start = ((), (), s32[]{:S(2)}) async-start(), calls=%async_computation.3 | async-start | bytes 327680 | tf_op jit(solution)/shard_map/while/body/eval_jaxpr/reduce_scatter | solution.py:102
  12.5 10.3 %collective-permute-start.1 = (bf16[128,1,256]{2,0,1:T(8,128)(2,1)S(1)}, bf16[128,1,256]{2,0,1:T(8,128)(2,1)S(1)}, u32[]{:S(2)}, u32[]{:S(2)}) collective-permute-start(bf16[128,1,256]{2,0,1:T(8,128)(2,1)S(1)} %slice.30), channel_id=1, source_target_pairs={{0,2},{2,4},{4,6},{6,8},{8,10},{10,12},{12,14},{1,3},{3,5},{5,7},{... | collective-permute-start | bytes 196616 | tf_op jit(solution)/shard_map/ppermute | solution.py:14
  17.5 6.9 %collective-permute-start = (bf16[128,1,256]{2,0,1:T(8,128)(2,1)S(1)}, bf16[128,1,256]{2,0,1:T(8,128)(2,1)S(1)}, u32[]{:S(2)}, u32[]{:S(2)}) collective-permute-start(bf16[128,1,256]{2,0,1:T(8,128)(2,1)S(1)} %slice.24), channel_id=1, source_target_pairs={{0,2},{2,4},{4,6},{6,8},{8,10},{10,12},{12,14},{1,3},{3,5},{5,7},{... | collective-permute-start | bytes 196616 | tf_op jit(solution)/shard_map/ppermute | solution.py:14
  21.2 1.0 %copy-start = (bf16[1024,1,256]{2,0,1:T(8,128)(2,1)S(1)}, bf16[1024,1,256]{2,0,1:T(8,128)(2,1)}, u32[]{:S(2)}) copy-start(bf16[1024,1,256]{2,0,1:T(8,128)(2,1)} %param.10) | copy-start | bytes 1572868
  21.4 1.3 %copy-start.10 = (s32[64]{0:T(128)S(1)}, s32[64]{0:T(128)}, u32[]{:S(2)}) copy-start(s32[64]{0:T(128)} %param.17) | copy-start | bytes 772
  24.4 1.0 %copy-start.4 = (bf16[1024,1,256]{2,0,1:T(8,128)(2,1)S(1)}, bf16[1024,1,256]{2,0,1:T(8,128)(2,1)}, u32[]{:S(2)}) copy-start(bf16[1024,1,256]{2,0,1:T(8,128)(2,1)} %param.12) | copy-start | bytes 1572868
  27.4 6.2 %copy-start.7 = (bf16[1,256,256]{2,1,0:T(8,128)(2,1)S(1)}, bf16[1,256,256]{2,1,0:T(8,128)(2,1)}, u32[]{:S(2)}) copy-start(bf16[1,256,256]{2,1,0:T(8,128)(2,1)} %param.15) | copy-start | bytes 393220
  35.4 23.7 %collective-permute-start.2 = (bf16[1,64,256]{2,1,0:T(8,128)(2,1)S(1)}, bf16[1,64,256]{2,1,0:T(8,128)(2,1)S(1)}, u32[]{:S(2)}, u32[]{:S(2)}) collective-permute-start(bf16[1,64,256]{2,1,0:T(8,128)(2,1)S(1)} %multiply_convert_fusion.4), channel_id=1, source_target_pairs={{0,8},{1,9},{2,10},{3,11},{4,12},{5,13},{6,14},{7,15},{16,24},{17,... | collective-permute-start | bytes 98312 | tf_op jit(solution)/shard_map/while/body/eval_jaxpr/ppermute | solution.py:14
  55.6 17.1 %collective-permute-start.3 = (bf16[1,2,64,256]{3,2,1,0:T(8,128)(2,1)S(1)}, bf16[1,2,64,256]{3,2,1,0:T(8,128)(2,1)S(1)}, u32[]{:S(2)}, u32[]{:S(2)}) collective-permute-start(bf16[1,2,64,256]{3,2,1,0:T(8,128)(2,1)S(1)} %multiply_convert_fusion.3), channel_id=1, source_target_pairs={{0,8},{1,9},{2,10},{3,11},{4,12},{5,13},{6,14},{7,15},{16,24},{17,... | collective-permute-start | bytes 196616 | tf_op jit(solution)/shard_map/while/body/eval_jaxpr/ppermute | solution.py:14
  88.4 1.9 %copy-start.8 = (f32[1,256]{1,0:T(1,128)S(1)}, f32[1,256]{1,0:T(1,128)}, u32[]{:S(2)}) copy-start(f32[1,256]{1,0:T(1,128)} %param.16) | copy-start | bytes 3076
Sparse Core Ops, SparseCore 0:
  12.6 20.9 reduce-scatter.2
  35.9 17.6 reduce-scatter.4
where the time goes:
time: 98.9 us; the launch traced here: 98.3 us
  blocking collectives  27.9 us (28%)
  waiting for transfers between devices  20.7 us (21%)
  starting transfers between devices  15.3 us (15%)
  between operations  13.8 us (14%)
  matrix products  9.19 us (9%)
  other arithmetic  7.46 us (8%)
  local copies, waits for them, and re-layouts  3.87 us (4%)
    ppermute x4, starting transfers between devices, from_behind(): return lax.ppermute(block, axis, route)  15.2 us
    reduce_scatter x1, waiting for transfers between devices, advance(): lax.psum_scatter(grad_in.astype(jnp.bfloat16), 'tok', scatter_dimension=2...  14.9 us
    all_gather x1, blocking collectives, advance(): lax.all_gather(own_in, 'tok', axis=2, tiled=True)  14.4 us
    all_gather x1, blocking collectives, advance(): lax.all_gather(own_out, 'tok', axis=1, tiled=True)  13.5 us
    reduce_scatter x1, waiting for transfers between devices, advance(): lax.psum_scatter(grad_out.astype(jnp.bfloat16), 'tok', scatter_dimension=...  5.84 us
    unnamed x22, local copies, waits for them, and re-layouts  2.46 us
  transfers between devices with their start and end apart: 6, of which 2 were waited for; matrix products, arithmetic and copies ran while one was open for 9% of the time, Pallas kernels for 0%

commit v1 on v0

--- a/solution.py
+++ b/solution.py
@@ -6,6 +6,27 @@
 
 BLOCK = 128
 EPSILON = 1e-06
+
+
+def ring_gather(value, axis, dim):
+    devices, index, rows = (lax.axis_size(axis), lax.axis_index(axis), value.shape[dim])
+    ahead = [(i, (i + 1) % devices) for i in range(devices)]
+    left = [(i, (i - 1) % devices) for i in range(devices)]
+    out = jnp.zeros((*value.shape[:dim], devices * rows, *value.shape[dim + 1 :]), value.dtype)
+    out = lax.dynamic_update_slice_in_dim(out, value, index * rows, axis=dim)
+    from_left = from_right = value
+    halfway = devices // 2
+    for step in range(1, halfway + 1):
+        from_left = lax.ppermute(from_left, axis, ahead)
+        out = lax.dynamic_update_slice_in_dim(
+            out, from_left, (index - step) % devices * rows, axis=dim
+        )
+        if step < devices - halfway:
+            from_right = lax.ppermute(from_right, axis, left)
+            out = lax.dynamic_update_slice_in_dim(
+                out, from_right, (index + step) % devices * rows, axis=dim
+            )
+    return out
 
 
 def from_behind(block, axis, distance):
@@ -114,7 +135,7 @@
         own_out = jnp.where(receiver, got_out, own_out)
         full_in, full_out = (
             lax.all_gather(own_in, "tok", axis=2, tiled=True),
-            lax.all_gather(own_out, "tok", axis=1, tiled=True),
+            ring_gather(own_out, "tok", 1),
         )
         return (full_in, full_out, own_in, own_out)
 

time: 98.9 us -> 86.9 us (0.88)
  blocking collectives: 27.9 us -> 13.9 us
  starting transfers between devices: 15.3 us -> 18.1 us
  waiting for transfers between devices: 20.7 us -> 18.9 us
    all_gather x1 -> x0, blocking collectives: 13.5 us -> none  [advance(): lax.all_gather(own_out, 'tok', axis=1, tiled=True)]
    reduce_scatter x1, waiting for transfers between devices: 14.9 us -> 5.2 us  [advance(): lax.psum_scatter(grad_in.astype(jnp.bfloat16), 'tok', scatter_dimension=2...]
    ppermute x4, waiting for transfers between devices: 0.01 us -> 3.39 us  [from_behind(): return lax.ppermute(block, axis, route)]
    reduce_scatter x1, waiting for transfers between devices: 5.84 us -> 9.15 us  [advance(): lax.psum_scatter(grad_out.astype(jnp.bfloat16), 'tok', scatter_dimension=...]
    ppermute x0 -> x3, starting transfers between devices: none -> 3.24 us  [the longest x1 3.24 us: ring_gather(): from_right = lax.ppermute(from_right, axis, left)]
    ppermute x0 -> x3, waiting for transfers between devices: none -> 1.12 us  [the longest x1 1.03 us: ring_gather(): from_right = lax.ppermute(from_right, axis, left)]
    unnamed x22 -> x24, local copies, waits for them, and re-layouts: 2.46 us -> 2.07 us
  transfers between devices with their start and end apart: 6 -> 9, of which waited for: 2 -> 6; matrix products, arithmetic and copies ran while one was open for 9% -> 12% of each run, Pallas kernels for 0% -> 0%
where the time goes in v1:
time: 86.9 us; the launch traced here: 86.2 us
  waiting for transfers between devices  18.9 us (22%)
  starting transfers between devices  18.1 us (21%)
  blocking collectives  13.9 us (16%)
  between operations  13.8 us (16%)
  matrix products  9.16 us (11%)
  other arithmetic  8.07 us (9%)
  local copies, waits for them, and re-layouts  4.3 us (5%)
    ppermute x4, starting transfers between devices, from_behind(): return lax.ppermute(block, axis, route)  14.7 us
    all_gather x1, blocking collectives, advance(): lax.all_gather(own_in, 'tok', axis=2, tiled=True)  13.9 us
    reduce_scatter x1, waiting for transfers between devices, advance(): lax.psum_scatter(grad_out.astype(jnp.bfloat16), 'tok', scatter_dimension=...  9.15 us
    reduce_scatter x1, waiting for transfers between devices, advance(): lax.psum_scatter(grad_in.astype(jnp.bfloat16), 'tok', scatter_dimension=2...  5.2 us
    ppermute x4, waiting for transfers between devices, from_behind(): return lax.ppermute(block, axis, route)  3.39 us
    ppermute x1, starting transfers between devices, ring_gather(): from_right = lax.ppermute(from_right, axis, left)  3.24 us
    unnamed x24, local copies, waits for them, and re-layouts  2.07 us
    dot_general x1, matrix products, attend_blocks(): jnp.einsum('nhqk,nkhd->nqhd', probabilities, window_values, preferred_ele...  1.94 us
  transfers between devices with their start and end apart: 9, of which 6 were waited for; matrix products, arithmetic and copies ran while one was open for 12% of the time, Pallas kernels for 0%

profile of v1, /device:TPU:0, one launch (start us, length us, event | category | flops | bytes accessed | tf_op | source)
XLA Modules:
  0.0 86.2 jit_solution(13657976858344189624)
XLA Ops:
  6.6 1.3 %fusion.28 = f32[1024]{0:T(1024)S(1)} fusion(bf16[1024,1,256]{2,0,1:T(8,128)(2,1)} %param.11), kind=kLoop, calls=%fused_computation.43 | loop fusion | flops 785408 | bytes 528384 | tf_op jit(solution)/shard_map/reduce_sum | solution.py:39
  7.9 1.2 %fusion.29 = bf16[1024,1,256]{2,0,1:T(8,128)(2,1)S(1)} fusion(bf16[1024,1,256]{2,0,1:T(8,128)(2,1)} %param.11, f32[1024]{0:T(1024)S(1)} %add_rsqrt_fusion.1), kind=kLoop, calls=%fused_computation.44 | loop fusion | flops 786432 | bytes 1052672 | tf_op jit(solution)/shard_map/convert_element_type | solution.py:92
  9.2 2.6 %conditional.1 = (bf16[1,2,256,256]{3,2,1,0:T(8,128)(2,1)S(1)}, bf16[1,256,256]{2,1,0:T(8,128)(2,1)S(1)}) conditional(s32[]{:T(128)} %convert_element_type.85, () %tuple.15, (f32[1024,1]{0,1:T(1,128)S(1)}, bf16[1024,1,256]{2,0,1:T(8,128)(2,1)S(1)}, bf16[1,256,256]{2,1,0:T(8,128)(2,1)S(1)}, bf16[1,2,256,256]{3,2,1,0:T(8,128)(2,1)S(1)}, ...), branch_computations={%region_3.0_spmd, %region_4.5_spmd} | conditional | flops 812908544 | bytes 11804688 | solution.py:113
  9.6 0.3 convolution_bitcast_fusion.1
  9.9 0.7 fusion.10
  10.6 0.5 convolution_bitcast_fusion.3
  11.1 0.6 convolution_bitcast_fusion.4
  11.8 0.6 copy-done.5
  12.5 4.9 %collective-permute-start.1 = (bf16[128,1,256]{2,0,1:T(8,128)(2,1)S(1)}, bf16[128,1,256]{2,0,1:T(8,128)(2,1)S(1)}, u32[]{:S(2)}, u32[]{:S(2)}) collective-permute-start(bf16[128,1,256]{2,0,1:T(8,128)(2,1)S(1)} %slice.30), channel_id=1, source_target_pairs={{0,2},{2,4},{4,6},{6,8},{8,10},{10,12},{12,14},{1,3},{3,5},{5,7},{... | collective-permute-start | bytes 196616 | tf_op jit(solution)/shard_map/ppermute | solution.py:35
  17.5 3.5 %collective-permute-start = (bf16[128,1,256]{2,0,1:T(8,128)(2,1)S(1)}, bf16[128,1,256]{2,0,1:T(8,128)(2,1)S(1)}, u32[]{:S(2)}, u32[]{:S(2)}) collective-permute-start(bf16[128,1,256]{2,0,1:T(8,128)(2,1)S(1)} %slice.24), channel_id=1, source_target_pairs={{0,2},{2,4},{4,6},{6,8},{8,10},{10,12},{12,14},{1,3},{3,5},{5,7},{... | collective-permute-start | bytes 196616 | tf_op jit(solution)/shard_map/ppermute | solution.py:35
  21.5 0.8 copy-done
  22.9 1.5 %fusion.23 = f32[8,128,256]{2,1,0:T(8,128)} fusion(bf16[8,128,256]{2,1,0:T(8,128)(2,1)S(1)} %bitcast.134, bf16[8,128,1,256]{3,1,0,2:T(8,128)(2,1)S(1)} %bitcast.133, bf16[8,128,1,256]{3,1,0,2:T(8,128)(2,1)S(1)} %bitcast.138, pred[128,256]{1,0:T(8,128)(4,1)S(1)} %get-tuple-element.73, pred[128,256]{1,0:T(8,128)(4,1)S(1)} %get-tuple-element.74, ...), kind=kOutput, calls=%fused_computation.34 | convolution fusion | flops 137101312 | bytes 2686984 | tf_op jit(solution)/shard_map/nqhd,nkhd->nhqk/dot_general | solution.py:72
  24.4 9.2 %reduce-scatter.3.cloned.1.call-done = bf16[1,64,256]{2,1,0:T(8,128)(2,1)} async-done(((bf16[1,256,256]{2,1,0:T(8,128)(2,1)}), bf16[1,64,256]{2,1,0:T(8,128)(2,1)}) %reduce-scatter.3.cloned.1.call-update) | async-done | bytes 32784 | tf_op jit(solution)/shard_map/while/body/eval_jaxpr/reduce_scatter | solution.py:126
  33.6 0.9 %multiply_reduce_fusion.4 = f32[64]{0:T(128)S(1)} fusion(bf16[1,64,256]{2,1,0:T(8,128)(2,1)} %reduce-scatter.3.cloned.1.call-done, bf16[1,256,256]{2,1,0:T(8,128)(2,1)S(1)} %copy-done.6, s32[]{:T(128)S(6)} %select_n.79), kind=kLoop, calls=%fused_computation.72 | loop fusion | flops 81856 | bytes 65796 | tf_op jit(solution)/shard_map/while/body/eval_jaxpr/reduce_sum | solution.py:48
  34.5 0.8 multiply_convert_fusion.4
  35.4 3.3 %collective-permute-start.2 = (bf16[1,64,256]{2,1,0:T(8,128)(2,1)S(1)}, bf16[1,64,256]{2,1,0:T(8,128)(2,1)S(1)}, u32[]{:S(2)}, u32[]{:S(2)}) collective-permute-start(bf16[1,64,256]{2,1,0:T(8,128)(2,1)S(1)} %multiply_convert_fusion.4), channel_id=1, source_target_pairs={{0,8},{1,9},{2,10},{3,11},{4,12},{5,13},{6,14},{7,15},{16,24},{17,... | collective-permute-start | bytes 98312 | tf_op jit(solution)/shard_map/while/body/eval_jaxpr/ppermute | solution.py:35
  38.7 1.5 %collective-permute-done.2 = bf16[1,64,256]{2,1,0:T(8,128)(2,1)S(1)} collective-permute-done((bf16[1,64,256]{2,1,0:T(8,128)(2,1)S(1)}, bf16[1,64,256]{2,1,0:T(8,128)(2,1)S(1)}, u32[]{:S(2)}, u32[]{:S(2)}) %collective-permute-start.2) | collective-permute-done | bytes 32800 | tf_op jit(solution)/shard_map/while/body/eval_jaxpr/ppermute | solution.py:35
  40.3 0.6 bitcast_dynamic-update-slice_fusion.3
  40.9 0.6 copy-done.7
  41.6 1.9 %fusion.32 = f32[8,256,128]{1,2,0:T(8,128)S(1)} fusion(bf16[8,128,1,256]{3,1,0,2:T(8,128)(2,1)S(1)} %bitcast.136, bf16[8,128,1,256]{3,1,0,2:T(8,128)(2,1)S(1)} %bitcast.137, f32[8,128,256]{2,1,0:T(8,128)} %fusion.23), kind=kOutput, calls=%fused_computation.49 | convolution fusion | flops 136840448 | bytes 3145728 | tf_op jit(solution)/shard_map/nhqk,nkhd->nqhd/dot_general | solution.py:84
  43.8 3.2 %collective-permute-start.4 = (bf16[1,64,256]{2,1,0:T(8,128)(2,1)}, bf16[1,64,256]{2,1,0:T(8,128)(2,1)S(1)}, u32[]{:S(2)}, u32[]{:S(2)}) collective-permute-start(bf16[1,64,256]{2,1,0:T(8,128)(2,1)} %get-tuple-element.68), channel_id=1, source_target_pairs={{0,6},{2,0},{4,2},{6,4},{1,7},{3,1},{5,3},{7,5},{8,14},{10,8},{12,... | collective-permute-start | bytes 98312 | tf_op jit(solution)/shard_map/while/body/eval_jaxpr/ppermute | solution.py:25
  47.2 0.8 bitcast_dynamic-update-slice_fusion.2
  48.0 1.0 %collective-permute-done.4 = bf16[1,64,256]{2,1,0:T(8,128)(2,1)S(1)} collective-permute-done((bf16[1,64,256]{2,1,0:T(8,128)(2,1)}, bf16[1,64,256]{2,1,0:T(8,128)(2,1)S(1)}, u32[]{:S(2)}, u32[]{:S(2)}) %collective-permute-start.4) | collective-permute-done | bytes 32800 | tf_op jit(solution)/shard_map/while/body/eval_jaxpr/ppermute | solution.py:25
  49.0 5.2 %reduce-scatter.5.cloned.1.call-done = bf16[1,2,64,256]{3,2,1,0:T(8,128)(2,1)} async-done(((bf16[1,2,256,256]{3,2,1,0:T(8,128)(2,1)}), bf16[1,2,64,256]{3,2,1,0:T(8,128)(2,1)}) %reduce-scatter.5.cloned.1.call-update) | async-done | bytes 65552 | tf_op jit(solution)/shard_map/while/body/eval_jaxpr/reduce_scatter | solution.py:123
  54.2 0.9 %multiply_reduce_fusion.3 = f32[2,64]{1,0:T(2,128)S(1)} fusion(bf16[1,2,64,256]{3,2,1,0:T(8,128)(2,1)} %reduce-scatter.5.cloned.1.call-done, bf16[1,2,256,256]{3,2,1,0:T(8,128)(2,1)S(1)} %copy-done.1, s32[]{:T(128)S(6)} %select_n.79), kind=kLoop, calls=%fused_computation.67 | loop fusion | flops 163712 | bytes 131588 | tf_op jit(solution)/shard_map/while/body/eval_jaxpr/reduce_sum | solution.py:48
  55.2 0.9 %multiply_convert_fusion.3 = bf16[1,2,64,256]{3,2,1,0:T(8,128)(2,1)S(1)} fusion(bf16[1,2,64,256]{3,2,1,0:T(8,128)(2,1)} %reduce-scatter.5.cloned.1.call-done, f32[2,64]{1,0:T(2,128)S(1)} %fusion.44, bf16[1,2,256,256]{3,2,1,0:T(8,128)(2,1)S(1)} %copy-done.1, s32[]{:T(128)S(6)} %select_n.79), kind=kLoop, calls=%fused_computation.66 | loop fusion | flops 163840 | bytes 197124 | tf_op jit(solution)/shard_map/while/body/eval_jaxpr/convert_element_type | solution.py:49
  56.2 3.0 %collective-permute-start.6 = (bf16[1,2,64,256]{3,2,1,0:T(8,128)(2,1)S(1)}, bf16[1,2,64,256]{3,2,1,0:T(8,128)(2,1)S(1)}, u32[]{:S(2)}, u32[]{:S(2)}) collective-permute-start(bf16[1,2,64,256]{3,2,1,0:T(8,128)(2,1)S(1)} %multiply_convert_fusion.3), channel_id=1, source_target_pairs={{0,8},{1,9},{2,10},{3,11},{4,12},{5,13},{6,14},{7,15},{16,24},{17,... | collective-permute-start | bytes 196616 | tf_op jit(solution)/shard_map/while/body/eval_jaxpr/ppermute | solution.py:35
  59.2 1.9 %collective-permute-done.6 = bf16[1,2,64,256]{3,2,1,0:T(8,128)(2,1)S(1)} collective-permute-done((bf16[1,2,64,256]{3,2,1,0:T(8,128)(2,1)S(1)}, bf16[1,2,64,256]{3,2,1,0:T(8,128)(2,1)S(1)}, u32[]{:S(2)}, u32[]{:S(2)}) %collective-permute-start.6) | collective-permute-done | bytes 65568 | tf_op jit(solution)/shard_map/while/body/eval_jaxpr/ppermute | solution.py:35
  61.1 13.9 %all_gather.4 = bf16[1,2,256,256]{3,2,1,0:T(8,128)(2,1)S(1)} all-gather(bf16[1,2,64,256]{3,2,1,0:T(8,128)(2,1)S(1)} %broadcast_select_fusion), channel_id=1, replica_groups=mesh['groups'=2,'span'=2,'tok'=4,'head'=2] {'tok'}, dimensions={2}, use_global_device_ids=true | all-gather | bytes 327680 | tf_op jit(solution)/shard_map/while/body/eval_jaxpr/all_gather | solution.py:137
  75.0 1.3 %convolution_bitcast_fusion.7 = f32[1024,1,256]{0,2,1:T(8,128)} fusion(bf16[1024,1,256]{2,0,1:T(8,128)(2,1)S(1)} %fusion.27, bf16[1,2,256,256]{3,2,1,0:T(8,128)(2,1)S(1)} %all_gather.4), kind=kOutput, calls=%fused_computation.31 | convolution fusion | flops 134217728 | bytes 1703936 | tf_op jit(solution)/shard_map/thd,hfd->thf/dot_general | solution.py:146
  76.3 1.9 %multiply_reduce_fusion = (f32[1024]{0:T(1024)S(1)}, f32[1,256,1024]{2,1,0:T(8,128)S(1)}) fusion(bf16[256,256]{1,0:T(8,128)(2,1)S(1)} %bitcast_dynamic-update-slice_fusion, f32[1024,1,256]{0,2,1:T(8,128)} %convolution_bitcast_fusion.7, bf16[1024,1,256]{2,0,1:T(8,128)(2,1)S(1)} %fusion.27, bf16[1,2,256,256]{3,2,1,0:T(8,128)(2,1)S(1)} %all_gather.4), kind=kOutput, calls=%fused_computation.54 | convolution fusion | flops 270531584 | bytes 2887680 | tf_op jit(solution)/shard_map/thf,hdf->thd/dot_general | solution.py:153
  78.4 1.0 %copy.20 = bf16[1024,1,256]{2,0,1:T(8,128)(2,1)} copy(bf16[1024,1,256]{0,2,1:T(8,128)(2,1)S(1)} %fusion.35) | data formatting | bytes 1048576 | tf_op jit(solution)/shard_map/convert_element_type | solution.py:170
  (58 shorter events, 2.3 us)
Async XLA Ops:
  6.5 2.7 %copy-start.3 = (bf16[1024,1,256]{2,0,1:T(8,128)(2,1)S(1)}, bf16[1024,1,256]{2,0,1:T(8,128)(2,1)}, u32[]{:S(2)}) copy-start(bf16[1024,1,256]{2,0,1:T(8,128)(2,1)} %param.12) | copy-start | bytes 1572868
  6.5 2.7 %copy-start.10 = (f32[1024,1]{0,1:T(1,128)S(1)}, f32[1024,1]{0,1:T(1,128)}, u32[]{:S(2)}) copy-start(f32[1024,1]{0,1:T(1,128)} %param.13) | copy-start | bytes 12292
  6.5 2.7 %copy-start.1 = (bf16[1,2,256,256]{3,2,1,0:T(8,128)(2,1)S(1)}, bf16[1,2,256,256]{3,2,1,0:T(8,128)(2,1)}, u32[]{:S(2)}) copy-start(bf16[1,2,256,256]{3,2,1,0:T(8,128)(2,1)} %param.14) | copy-start | bytes 786436
  6.5 2.7 %copy-start.6 = (bf16[1,256,256]{2,1,0:T(8,128)(2,1)S(1)}, bf16[1,256,256]{2,1,0:T(8,128)(2,1)}, u32[]{:S(2)}) copy-start(bf16[1,256,256]{2,1,0:T(8,128)(2,1)} %param.15) | copy-start | bytes 393220
  6.5 27.0 %reduce-scatter.3.cloned.1.call-start = ((), (), s32[]{:S(2)}) async-start(), calls=%async_computation.2 | async-start | bytes 163840 | tf_op jit(solution)/shard_map/while/body/eval_jaxpr/reduce_scatter | solution.py:126
  11.8 0.6 copy-start.5
  11.8 9.2 %copy-start.2 = (bf16[1,2,256,256]{3,2,1,0:T(8,128)(2,1)}, bf16[1,2,256,256]{3,2,1,0:T(8,128)(2,1)S(1)}, u32[]{:S(2)}) copy-start(bf16[1,2,256,256]{3,2,1,0:T(8,128)(2,1)S(1)} %get-tuple-element.45) | copy-start | bytes 786436
  12.5 41.7 %reduce-scatter.5.cloned.1.call-start = ((), (), s32[]{:S(2)}) async-start(), calls=%async_computation.3 | async-start | bytes 327680 | tf_op jit(solution)/shard_map/while/body/eval_jaxpr/reduce_scatter | solution.py:123
  12.5 10.4 %collective-permute-start.1 = (bf16[128,1,256]{2,0,1:T(8,128)(2,1)S(1)}, bf16[128,1,256]{2,0,1:T(8,128)(2,1)S(1)}, u32[]{:S(2)}, u32[]{:S(2)}) collective-permute-start(bf16[128,1,256]{2,0,1:T(8,128)(2,1)S(1)} %slice.30), channel_id=1, source_target_pairs={{0,2},{2,4},{4,6},{6,8},{8,10},{10,12},{12,14},{1,3},{3,5},{5,7},{... | collective-permute-start | bytes 196616 | tf_op jit(solution)/shard_map/ppermute | solution.py:35
  17.5 21.2 %collective-permute-start = (bf16[128,1,256]{2,0,1:T(8,128)(2,1)S(1)}, bf16[128,1,256]{2,0,1:T(8,128)(2,1)S(1)}, u32[]{:S(2)}, u32[]{:S(2)}) collective-permute-start(bf16[128,1,256]{2,0,1:T(8,128)(2,1)S(1)} %slice.24), channel_id=1, source_target_pairs={{0,2},{2,4},{4,6},{6,8},{8,10},{10,12},{12,14},{1,3},{3,5},{5,7},{... | collective-permute-start | bytes 196616 | tf_op jit(solution)/shard_map/ppermute | solution.py:35
  21.2 1.0 %copy-start = (bf16[1024,1,256]{2,0,1:T(8,128)(2,1)S(1)}, bf16[1024,1,256]{2,0,1:T(8,128)(2,1)}, u32[]{:S(2)}) copy-start(bf16[1024,1,256]{2,0,1:T(8,128)(2,1)} %param.10) | copy-start | bytes 1572868
  21.5 1.3 %copy-start.11 = (s32[64]{0:T(128)S(1)}, s32[64]{0:T(128)}, u32[]{:S(2)}) copy-start(s32[64]{0:T(128)} %param.17) | copy-start | bytes 772
  24.4 17.1 %copy-start.4 = (bf16[1024,1,256]{2,0,1:T(8,128)(2,1)S(1)}, bf16[1024,1,256]{2,0,1:T(8,128)(2,1)}, u32[]{:S(2)}) copy-start(bf16[1024,1,256]{2,0,1:T(8,128)(2,1)} %param.12) | copy-start | bytes 1572868
  35.4 4.9 %collective-permute-start.2 = (bf16[1,64,256]{2,1,0:T(8,128)(2,1)S(1)}, bf16[1,64,256]{2,1,0:T(8,128)(2,1)S(1)}, u32[]{:S(2)}, u32[]{:S(2)}) collective-permute-start(bf16[1,64,256]{2,1,0:T(8,128)(2,1)S(1)} %multiply_convert_fusion.4), channel_id=1, source_target_pairs={{0,8},{1,9},{2,10},{3,11},{4,12},{5,13},{6,14},{7,15},{16,24},{17,... | collective-permute-start | bytes 98312 | tf_op jit(solution)/shard_map/while/body/eval_jaxpr/ppermute | solution.py:35
  40.9 0.6 copy-start.7
  40.9 6.3 %collective-permute-start.3 = (bf16[1,64,256]{2,1,0:T(8,128)(2,1)}, bf16[1,64,256]{2,1,0:T(8,128)(2,1)}, u32[]{:S(2)}, u32[]{:S(2)}) collective-permute-start(bf16[1,64,256]{2,1,0:T(8,128)(2,1)} %get-tuple-element.68), channel_id=1, source_target_pairs={{0,2},{2,4},{4,6},{6,0},{1,3},{3,5},{5,7},{7,1},{8,10},{10,12},{12... | collective-permute-start | bytes 98312 | tf_op jit(solution)/shard_map/while/body/eval_jaxpr/ppermute | solution.py:20
  43.5 3.7 %copy-start.8 = (bf16[256,256]{1,0:T(8,128)(2,1)S(1)}, bf16[256,256]{1,0:T(8,128)(2,1)}, u32[]{:S(2)}) copy-start(bf16[256,256]{1,0:T(8,128)(2,1)} %copy-done.7) | copy-start | bytes 393220
  43.8 5.2 %collective-permute-start.4 = (bf16[1,64,256]{2,1,0:T(8,128)(2,1)}, bf16[1,64,256]{2,1,0:T(8,128)(2,1)S(1)}, u32[]{:S(2)}, u32[]{:S(2)}) collective-permute-start(bf16[1,64,256]{2,1,0:T(8,128)(2,1)} %get-tuple-element.68), channel_id=1, source_target_pairs={{0,6},{2,0},{4,2},{6,4},{1,7},{3,1},{5,3},{7,5},{8,14},{10,8},{12,... | collective-permute-start | bytes 98312 | tf_op jit(solution)/shard_map/while/body/eval_jaxpr/ppermute | solution.py:25
  47.2 12.0 %collective-permute-start.5 = (bf16[1,64,256]{2,1,0:T(8,128)(2,1)}, bf16[1,64,256]{2,1,0:T(8,128)(2,1)S(1)}, u32[]{:S(2)}, u32[]{:S(2)}) collective-permute-start(bf16[1,64,256]{2,1,0:T(8,128)(2,1)} %collective-permute-done.3), channel_id=1, source_target_pairs={{0,2},{2,4},{4,6},{6,0},{1,3},{3,5},{5,7},{7,1},{8,10},{10,12},{12... | collective-permute-start | bytes 98312 | tf_op jit(solution)/shard_map/while/body/eval_jaxpr/ppermute | solution.py:20
  56.2 4.9 %collective-permute-start.6 = (bf16[1,2,64,256]{3,2,1,0:T(8,128)(2,1)S(1)}, bf16[1,2,64,256]{3,2,1,0:T(8,128)(2,1)S(1)}, u32[]{:S(2)}, u32[]{:S(2)}) collective-permute-start(bf16[1,2,64,256]{3,2,1,0:T(8,128)(2,1)S(1)} %multiply_convert_fusion.3), channel_id=1, source_target_pairs={{0,8},{1,9},{2,10},{3,11},{4,12},{5,13},{6,14},{7,15},{16,24},{17,... | collective-permute-start | bytes 196616 | tf_op jit(solution)/shard_map/while/body/eval_jaxpr/ppermute | solution.py:35
  76.3 1.9 %copy-start.9 = (f32[1,256]{1,0:T(1,128)S(1)}, f32[1,256]{1,0:T(1,128)}, u32[]{:S(2)}) copy-start(f32[1,256]{1,0:T(1,128)} %param.16) | copy-start | bytes 3076
Sparse Core Ops, SparseCore 0:
  12.6 20.9 reduce-scatter.2
  35.9 18.2 reduce-scatter.4
